TPU v7x, 32 devices: a whole 2x2x4 slice. The times are simulated.
32 devices in a mesh: day: 16 (over z, x, core), pair: 2 (over y).
Axes of the slice: x: 2, y: 2, z: 4, core: 2. Of those that a mesh axis runs over, the one named last changes fastest.
Arguments:
- spectra: bfloat16 [64, 128, 1024], P('day', 'pair'), may hold values from -4 to 4
- pair_list: int32 [1024, 2], P('pair'), may hold values from 0 to 127, as said below
- mask: int32 [64, 128], P('day'), may hold values from 0 to 1
Outputs:
- linear_stack: float32 [401, 1024], P(None, ('pair', 'day'))
- weighted_stack: float32 [401, 1024], P(None, ('pair', 'day'))
Inputs may be any that keep to these rules, and one draw needn't show every extreme that they name: `pair_list`: the two stations of a pair differ.
All inputs are finite; a program needn't handle non-finite values.
Results may differ from a plain program's by a relative error of at most 0.0039.
Values may be sent and summed in bfloat16 or wider, within the bound.
A program may use at most 64 MiB of HBM per device.

v0:
```python
import math

import jax
import jax.numpy as jnp
from jax import lax
from jax.sharding import PartitionSpec as P

F = 512
MAXLAG = 200
LAGS = 401


def lag_table():
    lag = jnp.arange(LAGS, dtype=jnp.int32) - MAXLAG
    freq = jnp.arange(F, dtype=jnp.int32)
    phase = jnp.mod(lag[:, None] * freq[None, :], 2 * F).astype(jnp.float32) * (math.pi / F)
    scale = 1.0 / math.sqrt(F)
    cosine = jnp.cos(phase) * scale
    sine = jnp.sin(phase) * scale
    upper = jnp.concatenate([cosine, -sine], 1)
    lower = jnp.concatenate([sine, cosine], 1)
    return jnp.concatenate([upper, lower], 0).astype(jnp.bfloat16)


def per_device(spectra, pair_list, mask):
    gathered = lax.all_gather(spectra, "pair", axis=1, tiled=True)
    station_count = gathered.shape[1]
    pair_rows = pair_list.shape[0]
    first = pair_list[:, 0]
    second = pair_list[:, 1]
    column = lax.broadcasted_iota(jnp.int32, (pair_rows, station_count), 1)
    pick_first = (first[:, None] == column).astype(jnp.float32)
    pick_second = (second[:, None] == column).astype(jnp.float32)
    mask_float = mask.astype(jnp.float32)
    weights = jnp.einsum("ds,ps->dp", mask_float, pick_first) * jnp.einsum(
        "ds,ps->dp", mask_float, pick_second
    )
    count_local = jnp.sum(weights, 0, keepdims=True)
    groups = lax.axis_size("day")
    owned = pair_rows // groups
    start = lax.axis_index("day") * owned
    table = lag_table()

    def one_day(carry, inputs):
        day_spec, weight = inputs
        left = jnp.take(day_spec, first, axis=0).astype(jnp.float32)
        right = jnp.take(day_spec, second, axis=0).astype(jnp.float32)
        half = left.shape[1] // 2
        left_re, left_im = (left[:, :half], left[:, half:])
        right_re, right_im = (right[:, :half], right[:, half:])
        cross_re = left_re * right_re + left_im * right_im
        cross_im = left_im * right_re - left_re * right_im
        cross = jnp.concatenate([cross_re, cross_im], 1).astype(jnp.bfloat16)
        analytic = lax.dot_general(
            table, cross, (((1,), (1,)), ((), ())), preferred_element_type=jnp.float32
        )
        trace = analytic[:LAGS]
        hilbert = analytic[LAGS:]
        amplitude = jnp.sqrt(trace * trace + hilbert * hilbert)
        inverse = 1.0 / jnp.maximum(amplitude, 0.5)
        lin_sum, real_sum, imag_sum = carry
        lin_sum = lin_sum + weight[None, :] * trace
        real_sum = real_sum + weight[None, :] * (trace * inverse)
        imag_sum = imag_sum + weight[None, :] * (hilbert * inverse)
        return ((lin_sum, real_sum, imag_sum), None)

    zeros = jnp.zeros((LAGS, pair_rows), jnp.float32)
    (lin_sum, real_sum, imag_sum), _ = lax.scan(one_day, (zeros, zeros, zeros), (gathered, weights))
    lin_all, real_all, imag_all, count_all = lax.psum(
        (lin_sum, real_sum, imag_sum, count_local), "day"
    )
    count_own = lax.dynamic_slice_in_dim(count_all, start, owned, 1)
    lin_own = lax.dynamic_slice_in_dim(lin_all, start, owned, 1)
    real_own = lax.dynamic_slice_in_dim(real_all, start, owned, 1)
    imag_own = lax.dynamic_slice_in_dim(imag_all, start, owned, 1)
    linear_stack = lin_own / count_own
    weighted_stack = (
        linear_stack * (real_own * real_own + imag_own * imag_own) / (count_own * count_own)
    )
    return (linear_stack, weighted_stack)


def solution(mesh):
    in_specs = (P("day", "pair", None), P("pair", None), P("day", None))
    out_specs = (P(None, ("pair", "day")), P(None, ("pair", "day")))
    return jax.shard_map(
        per_device, mesh=mesh, in_specs=in_specs, out_specs=out_specs, check_vma=False
    )
```

profile of v0, /device:TPU:0, one launch (start us, length us, event | category | flops | bytes accessed | tf_op | source)
XLA Modules:
  0.0 200.7 jit_solution(10898020374540674718)
XLA Ops:
  7.2 0.7 all-gather.2.cloned.1.call-update
  8.0 3.7 %negate_convert_fusion = (bf16[401,512]{1,0:T(8,128)(2,1)S(1)}, bf16[401,512]{1,0:T(8,128)(2,1)S(1)}, bf16[401,512]{1,0:T(8,128)(2,1)S(1)}) fusion(s32[401]{0:T(512)S(1)} %iota_add_fusion), kind=kLoop, calls=%fused_computation.31 | loop fusion | flops 4106240 | bytes 1233476 | tf_op jit(solution)/shard_map/convert.7
  11.7 1.4 maximum_maximum_fusion
  13.4 0.3 fusion.18
  13.7 19.9 %all-gather.2.cloned.1.call-done = bf16[4,128,1024]{2,1,0:T(8,128)(2,1)} async-done(((bf16[4,64,1024]{2,1,0:T(8,128)(2,1)}), bf16[4,128,1024]{2,1,0:T(8,128)(2,1)}) %all-gather.2.cloned.1.call-update) | async-done | bytes 1048592 | tf_op jit(solution)/shard_map/all_gather | solution.py:26
  33.6 48.9 %while.15 = (s32[]{:T(128)}, f32[401,512]{1,0:T(8,128)}, f32[401,512]{1,0:T(8,128)}, f32[401,512]{1,0:T(8,128)}, f32[4,512]{1,0:T(4,128)S(1)}, /*index=5*/bf16[4...) while((s32[]{:T(128)}, f32[401,512]{1,0:T(8,128)}, ...), condition=%wide.region_1.3_spmd.clone, body=%wide.region_0.2_spmd.clone.sunk | while | flops 850545664 | bytes 46903560 | solution.py:68
  33.6 1.0 dynamic-slice_bitcast_fusion.2
  34.6 2.1 %gather_fusion = bf16[512,1024]{1,0:T(8,128)(2,1)S(1)} fusion(bf16[128,1024]{1,0:T(8,128)(2,1)S(1)} %dynamic-slice_bitcast_fusion.2, s32[1024]{0:T(1024)S(1)} %pad_clamp_fusion.4), kind=kCustom, calls=%fused_computation.1.clone.clone.1 | custom fusion | bytes 2099200 | tf_op jit(solution)/shard_map/while/body/eval_jaxpr/jit(_take)/gather | solution.py:47
  36.9 2.1 %gather_fusion.1 = bf16[512,1024]{1,0:T(8,128)(2,1)S(1)} fusion(bf16[128,1024]{1,0:T(8,128)(2,1)S(1)} %dynamic-slice_bitcast_fusion.2, s32[1024]{0:T(1024)S(1)} %pad_clamp_fusion.5), kind=kCustom, calls=%fused_computation.clone.clone.1 | custom fusion | bytes 2099200 | tf_op jit(solution)/shard_map/while/body/eval_jaxpr/jit(_take)/gather | solution.py:46
  39.2 0.6 add_convert_fusion.2
  39.8 0.8 copy-done.6
  40.6 1.0 convolution_bitcast_fusion.2
  42.0 1.8 select_add_fusion.4
  43.8 0.9 copy-done.1
  44.7 0.3 copy-done.3
  45.0 1.0 dynamic-slice_bitcast_fusion.2
  46.0 2.1 %gather_fusion = bf16[512,1024]{1,0:T(8,128)(2,1)S(1)} fusion(bf16[128,1024]{1,0:T(8,128)(2,1)S(1)} %dynamic-slice_bitcast_fusion.2, s32[1024]{0:T(1024)S(1)} %pad_clamp_fusion.4), kind=kCustom, calls=%fused_computation.1.clone.clone.1 | custom fusion | bytes 2099200 | tf_op jit(solution)/shard_map/while/body/eval_jaxpr/jit(_take)/gather | solution.py:47
  48.3 2.1 %gather_fusion.1 = bf16[512,1024]{1,0:T(8,128)(2,1)S(1)} fusion(bf16[128,1024]{1,0:T(8,128)(2,1)S(1)} %dynamic-slice_bitcast_fusion.2, s32[1024]{0:T(1024)S(1)} %pad_clamp_fusion.5), kind=kCustom, calls=%fused_computation.clone.clone.1 | custom fusion | bytes 2099200 | tf_op jit(solution)/shard_map/while/body/eval_jaxpr/jit(_take)/gather | solution.py:46
  50.6 0.6 add_convert_fusion.2
  51.1 0.8 copy-done.6
  52.0 1.0 convolution_bitcast_fusion.2
  53.4 2.9 %select_add_fusion.4 = (f32[401,512]{1,0:T(8,128)}, f32[401,512]{1,0:T(8,128)S(1)}, f32[401,512]{1,0:T(8,128)S(1)}) fusion(f32[401,512]{1,0:T(8,128)} %get-tuple-element.213, f32[802,512]{1,0:T(8,128)S(1)} %convolution_bitcast_fusion.2, f32[512]{0:T(512)S(1)} %bitcast.26, pred[]{:T(512)S(6)} %compare.4, f32[401,512]{1,0:T(8,128)S(1)} %copy-done.2, ...), kind=kLoop, calls=%fused_computation.10.clone.1 | loop fusion | flops 3284992 | bytes 6572033 | tf_op jit(solution)/shard_map/while/body/eval_jaxpr/add | solution.py:64
  56.3 0.9 copy-done.1
  57.2 0.3 copy-done.3
  57.5 1.0 dynamic-slice_bitcast_fusion.2
  58.5 2.1 %gather_fusion = bf16[512,1024]{1,0:T(8,128)(2,1)S(1)} fusion(bf16[128,1024]{1,0:T(8,128)(2,1)S(1)} %dynamic-slice_bitcast_fusion.2, s32[1024]{0:T(1024)S(1)} %pad_clamp_fusion.4), kind=kCustom, calls=%fused_computation.1.clone.clone.1 | custom fusion | bytes 2099200 | tf_op jit(solution)/shard_map/while/body/eval_jaxpr/jit(_take)/gather | solution.py:47
  60.8 2.1 %gather_fusion.1 = bf16[512,1024]{1,0:T(8,128)(2,1)S(1)} fusion(bf16[128,1024]{1,0:T(8,128)(2,1)S(1)} %dynamic-slice_bitcast_fusion.2, s32[1024]{0:T(1024)S(1)} %pad_clamp_fusion.5), kind=kCustom, calls=%fused_computation.clone.clone.1 | custom fusion | bytes 2099200 | tf_op jit(solution)/shard_map/while/body/eval_jaxpr/jit(_take)/gather | solution.py:46
  63.1 0.6 add_convert_fusion.2
  63.7 0.8 copy-done.6
  64.5 1.0 convolution_bitcast_fusion.2
  65.9 2.9 %select_add_fusion.4 = (f32[401,512]{1,0:T(8,128)}, f32[401,512]{1,0:T(8,128)S(1)}, f32[401,512]{1,0:T(8,128)S(1)}) fusion(f32[401,512]{1,0:T(8,128)} %get-tuple-element.213, f32[802,512]{1,0:T(8,128)S(1)} %convolution_bitcast_fusion.2, f32[512]{0:T(512)S(1)} %bitcast.26, pred[]{:T(512)S(6)} %compare.4, f32[401,512]{1,0:T(8,128)S(1)} %copy-done.2, ...), kind=kLoop, calls=%fused_computation.10.clone.1 | loop fusion | flops 3284992 | bytes 6572033 | tf_op jit(solution)/shard_map/while/body/eval_jaxpr/add | solution.py:64
  68.8 0.9 copy-done.1
  69.7 0.3 copy-done.3
  70.0 1.0 dynamic-slice_bitcast_fusion.2
  71.0 2.1 %gather_fusion = bf16[512,1024]{1,0:T(8,128)(2,1)S(1)} fusion(bf16[128,1024]{1,0:T(8,128)(2,1)S(1)} %dynamic-slice_bitcast_fusion.2, s32[1024]{0:T(1024)S(1)} %pad_clamp_fusion.4), kind=kCustom, calls=%fused_computation.1.clone.clone.1 | custom fusion | bytes 2099200 | tf_op jit(solution)/shard_map/while/body/eval_jaxpr/jit(_take)/gather | solution.py:47
  73.3 2.1 %gather_fusion.1 = bf16[512,1024]{1,0:T(8,128)(2,1)S(1)} fusion(bf16[128,1024]{1,0:T(8,128)(2,1)S(1)} %dynamic-slice_bitcast_fusion.2, s32[1024]{0:T(1024)S(1)} %pad_clamp_fusion.5), kind=kCustom, calls=%fused_computation.clone.clone.1 | custom fusion | bytes 2099200 | tf_op jit(solution)/shard_map/while/body/eval_jaxpr/jit(_take)/gather | solution.py:46
  75.6 0.6 add_convert_fusion.2
  76.2 0.8 copy-done.6
  77.0 1.0 convolution_bitcast_fusion.2
  78.4 2.9 %select_add_fusion.4 = (f32[401,512]{1,0:T(8,128)}, f32[401,512]{1,0:T(8,128)S(1)}, f32[401,512]{1,0:T(8,128)S(1)}) fusion(f32[401,512]{1,0:T(8,128)} %get-tuple-element.213, f32[802,512]{1,0:T(8,128)S(1)} %convolution_bitcast_fusion.2, f32[512]{0:T(512)S(1)} %bitcast.26, pred[]{:T(512)S(6)} %compare.4, f32[401,512]{1,0:T(8,128)S(1)} %copy-done.2, ...), kind=kLoop, calls=%fused_computation.10.clone.1 | loop fusion | flops 3284992 | bytes 6572033 | tf_op jit(solution)/shard_map/while/body/eval_jaxpr/add | solution.py:64
  81.3 0.9 copy-done.1
  82.2 0.3 copy-done.3
  82.5 2.6 %copy.5 = f32[401,512]{0,1:T(8,128)} copy(f32[401,512]{1,0:T(8,128)} %get-tuple-element.52) | data formatting | bytes 1642496 | tf_op jit(solution)/shard_map/while | solution.py:68
  85.1 1.3 copy.6
  86.4 1.4 copy.7
  87.8 33.9 %psum.29 = f32[1,512]{1,0:T(1,128)S(1)} all-reduce(f32[1,512]{1,0:T(1,128)S(1)} %bitcast.28), channel_id=1, replica_groups=mesh['day'=16,'pair'=2] {'day'}, use_global_device_ids=true, to_apply=%region_4.6 | all-reduce | flops 512 | bytes 4096 | tf_op jit(solution)/shard_map/psum | solution.py:69
  121.8 70.4 %all-reduce.3.cloned.1.call-done = (f32[401,512]{0,1:T(8,128)}, f32[401,512]{0,1:T(8,128)}, f32[401,512]{0,1:T(8,128)}) async-done(((f32[401,512]{0,1:T(8,128)}, f32[401,512]{0,1:T(8,128)}, f32[401,512]{0,1:T(8,128)}), (f32[401,512]{0,1:T(8,128)}, f32[401,512]{0,1:T(8,128)}, f32[401,512]{0,1:T(8,128)})) %all-reduce.3.cloned.1.call-update) | async-done | bytes 2463760 | tf_op jit(solution)/shard_map/psum | solution.py:69
  192.2 1.6 multiply_divide_fusion
  (74 shorter events, 3.6 us)
Async XLA Ops:
  7.2 26.4 %all-gather.2.cloned.1.call-start = ((), (), s32[]{:S(2)}) async-start(), calls=%async_computation | async-start | bytes 1572864 | tf_op jit(solution)/shard_map/all_gather | solution.py:26
  7.9 5.3 %copy-start.7 = (s32[512,2]{0,1:T(2,128)S(1)}, s32[512,2]{0,1:T(2,128)}, u32[]{:S(2)}) copy-start(s32[512,2]{0,1:T(2,128)} %param.8) | copy-start | bytes 12292
  7.9 5.3 %copy-start.8 = (s32[4,128]{1,0:T(4,128)S(1)}, s32[4,128]{1,0:T(4,128)}, u32[]{:S(2)}) copy-start(s32[4,128]{1,0:T(4,128)} %param.9) | copy-start | bytes 6148
  7.9 184.3 %all-reduce.3.cloned.1.call-start = ((), (), s32[]{:S(2)}) async-start(), calls=%async_computation.1 | async-start | bytes 6291456 | tf_op jit(solution)/shard_map/psum | solution.py:69
  39.2 1.4 copy-start.6
  40.6 1.1 copy-start
  40.6 1.4 copy-start.2
  43.8 0.9 copy-start.1
  43.8 1.2 copy-start.3
  50.5 1.4 copy-start.6
  52.0 1.1 copy-start
  52.0 1.4 copy-start.2
  56.3 0.9 copy-start.1
  56.3 1.2 copy-start.3
  63.1 1.4 copy-start.6
  64.5 1.1 copy-start
  64.5 1.4 copy-start.2
  68.8 0.9 copy-start.1
  68.8 1.2 copy-start.3
  75.6 1.4 copy-start.6
  77.0 1.1 copy-start
  77.0 1.4 copy-start.2
  81.3 0.9 copy-start.1
  81.3 1.2 copy-start.3
  82.5 2.6 %copy-start.4 = (f32[401,512]{1,0:T(8,128)S(1)}, f32[401,512]{1,0:T(8,128)}, u32[]{:S(2)}) copy-start(f32[401,512]{1,0:T(8,128)} %get-tuple-element.53) | copy-start | bytes 2463748
  82.5 3.9 %copy-start.5 = (f32[401,512]{1,0:T(8,128)S(1)}, f32[401,512]{1,0:T(8,128)}, u32[]{:S(2)}) copy-start(f32[401,512]{1,0:T(8,128)} %get-tuple-element.54) | copy-start | bytes 2463748
Sparse Core Ops, SparseCore 0:
  9.5 23.9 all-gather.1
  87.9 104.2 all-reduce.2
where the time goes:
time: 201 us
  waiting for transfers between devices  91 us (45%)
  local copies, waits for them, and re-layouts  35.1 us (17%)
  blocking collectives  33.9 us (17%)
  other arithmetic  21.4 us (11%)
  between operations  14.1 us (7%)
  matrix products  4.71 us (2%)
    psum x1, waiting for transfers between devices, per_device(): lax.psum((lin_sum, real_sum, imag_sum, count_local), 'day')  70.4 us
    psum x1, blocking collectives, per_device(): lax.psum((lin_sum, real_sum, imag_sum, count_local), 'day')  33.9 us
    all_gather x1, waiting for transfers between devices, per_device(): gathered = lax.all_gather(spectra, 'pair', axis=1, tiled=True)  19.9 us
    add x4, other arithmetic, one_day(): imag_sum = imag_sum + weight[None, :] * (hilbert * inverse)  10.5 us
    while x40, local copies, waits for them, and re-layouts  9.38 us
    gather x4, local copies, waits for them, and re-layouts, one_day(): left = jnp.take(day_spec, first, axis=0).astype(jnp.float32)  8.23 us
    gather x4, local copies, waits for them, and re-layouts, one_day(): right = jnp.take(day_spec, second, axis=0).astype(jnp.float32)  8.23 us
    another operation x5, other arithmetic  6.04 us
  transfers between devices with their start and end apart: 2, of which 2 were waited for; matrix products, arithmetic and copies ran while one was open for 3% of the time, Pallas kernels for 0%

commit v1 on v0

v1 whole, which is shorter than its diff:
```python
import functools
import math

import jax
import jax.numpy as jnp
import ml_dtypes
import numpy as np
from jax import lax
from jax.experimental import pallas as pl
from jax.experimental.pallas import tpu as pltpu
from jax.sharding import PartitionSpec as P

F = 512
MAXLAG = 200
LAGS = 401
LANES = 512
FULL = 384
PACKED = 1280
MESH = pl.DeviceIdType.MESH


def lag_table():
    lag = np.arange(LAGS) - MAXLAG
    freq = np.arange(F)
    phase = np.mod(lag[:, None] * freq[None, :], 2 * F) * (math.pi / F)
    cosine = np.cos(phase) / math.sqrt(F)
    sine = np.sin(phase) / math.sqrt(F)
    table = np.zeros((2 * F, 2 * LANES), np.float32)
    table[:F, :LAGS] = cosine.T
    table[F:, :LAGS] = -sine.T
    table[:F, LANES : LANES + LAGS] = sine.T
    table[F:, LANES : LANES + LAGS] = cosine.T
    return table.astype(ml_dtypes.bfloat16)


def streams_of(steps):
    straight = list(range(steps))
    turned = [0] + straight[2:] + [1] if steps > 2 else straight
    half = PACKED // 2
    return [(0, half, straight), (half, half, turned)]


def kernel(
    groups, halves, spectra, pairs, mask, table, lin_out, wgt_out,
    spec_all, table_v, pick, acc, tail, work, outbox, inbox,
    load_sem, gsend, grecv, rsend, rrecv,
):
    days, local, _ = spectra.shape
    rows = acc.shape[0]
    own = rows // groups
    steps = groups.bit_length() - 1
    streams = streams_of(steps)
    me = lax.axis_index("day")
    side = lax.axis_index("pair")

    def partner(bit):
        size = 1 << bit
        mine = lax.rem(lax.div(me, size), 2)
        return mine, me + (1 - 2 * mine) * size

    mine_rows = pl.ds(pl.multiple_of(side * local, local), local)
    loads = [
        pltpu.make_async_copy(spectra, spec_all.at[:, mine_rows, :], load_sem.at[0]),
        pltpu.make_async_copy(table, table_v, load_sem.at[1]),
    ]
    for copy in loads:
        copy.start()

    barrier = pltpu.get_barrier_semaphore()
    for off in range(1, halves):
        pl.semaphore_signal(
            barrier, inc=1, device_id=(me, lax.rem(side + off, halves)), device_id_type=MESH
        )
    for bit in range(steps):
        pl.semaphore_signal(barrier, inc=1, device_id=(partner(bit)[1], side), device_id_type=MESH)
    pl.semaphore_wait(barrier, halves - 1 + steps)

    def gather(day, off):
        return pltpu.make_async_remote_copy(
            src_ref=spectra.at[day],
            dst_ref=spec_all.at[day, mine_rows, :],
            send_sem=gsend.at[day, off - 1],
            recv_sem=grecv.at[day, off - 1],
            device_id=(me, lax.rem(side + off, halves)),
            device_id_type=MESH,
        )

    for day in range(days):
        for off in range(1, halves):
            gather(day, off).start()

    stations = local * halves
    row = lax.broadcasted_iota(jnp.int32, (stations, rows), 0)
    for end in range(2):
        hot = (pairs[end : end + 1, :] == row).astype(jnp.float32)
        pick[end] = hot.T
    acc[...] = jnp.zeros_like(acc)
    tail[...] = jnp.zeros_like(tail)
    live = mask[...].astype(jnp.float32)
    seen = [
        lax.dot_general(
            pick[end], live, (((1,), (1,)), ((), ())), preferred_element_type=jnp.float32
        )
        for end in range(2)
    ]
    count = jnp.sum(seen[0] * seen[1], 1, keepdims=True)
    lane = lax.broadcasted_iota(jnp.int32, (rows, 128), 1)
    tail[0] = jnp.where(lane == 96, count, 0.0)
    for copy in loads:
        copy.wait()

    block = min(rows, 256)

    def one_day(day, carry):
        for off in range(1, halves):
            gather(day, off).wait()
        today = mask[pl.ds(day, 1), :].astype(jnp.float32)
        spec = spec_all[day]
        for start in range(0, rows, block):
            here = pl.ds(start, block)
            left, right = (
                jnp.dot(
                    (pick[end, here] * today).astype(jnp.bfloat16),
                    spec,
                    preferred_element_type=jnp.float32,
                )
                for end in range(2)
            )
            left_re, left_im = left[:, :F], left[:, F:]
            right_re, right_im = right[:, :F], right[:, F:]
            cross = jnp.concatenate(
                [
                    (left_re * right_re + left_im * right_im).astype(jnp.bfloat16),
                    (left_im * right_re - left_re * right_im).astype(jnp.bfloat16),
                ],
                1,
            )
            analytic = jnp.dot(cross, table_v[...], preferred_element_type=jnp.float32)
            trace, hilbert = analytic[:, :LANES], analytic[:, LANES:]
            inverse = lax.rsqrt(jnp.maximum(trace * trace + hilbert * hilbert, 0.25))
            for n, value in enumerate((trace, trace * inverse, hilbert * inverse)):
                acc[here, n * FULL : (n + 1) * FULL] += value[:, :FULL]
                tail[n, here, :] += value[:, FULL:]
        return carry

    lax.fori_loop(0, days, one_day, 0)
    acc[:, 3 * FULL :] = tail[0] + pltpu.roll(tail[1], 32, 1) + pltpu.roll(tail[2], 64, 1)

    def exchange(s, k):
        blocks = groups >> (k + 1)
        base = groups - (groups >> k)
        return pltpu.make_async_remote_copy(
            src_ref=outbox.at[s, pl.ds(base, blocks)],
            dst_ref=inbox.at[s, pl.ds(base, blocks)],
            send_sem=rsend.at[s, k],
            recv_sem=rrecv.at[s, k],
            device_id=(partner(streams[s][2][k])[1], side),
            device_id_type=MESH,
        )

    def first_rows(s, i, bit):
        order = streams[s][2]
        natural = sum(((i >> (steps - 1 - n)) & 1) << order[n] for n in range(1, steps))
        return pl.ds(pl.multiple_of((natural + bit) * own, own), own)

    for k in range(steps + 1):
        for s, (lane0, width, order) in enumerate(streams):
            lanes = pl.ds(lane0, width)
            if k:
                mine, _ = partner(order[k - 1])
                blocks = groups >> k
                base = groups - (groups >> (k - 1))
                before = groups - (groups >> (k - 2)) if k > 1 else 0
                exchange(s, k - 1).wait_recv()
                for i in range(blocks):
                    if k == 1:
                        kept = acc[first_rows(s, i, mine), lanes]
                    else:
                        kept = work[s, before + mine * blocks + i]
                    work[s, base + i] = kept + inbox[s, base + i].astype(jnp.float32)
            if k < steps:
                mine, _ = partner(order[k])
                blocks = groups >> (k + 1)
                base = groups - (groups >> k)
                before = groups - (groups >> (k - 1)) if k else 0
                for i in range(blocks):
                    if k == 0:
                        sent = acc[first_rows(s, i, 1 - mine), lanes]
                    else:
                        sent = work[s, before + (1 - mine) * blocks + i]
                    outbox[s, base + i] = sent.astype(jnp.bfloat16)
                exchange(s, k).start()
    for s in range(len(streams)):
        for k in range(steps):
            exchange(s, k).wait_send()

    last = groups - 2
    whole = jnp.concatenate([work[s, last] for s in range(len(streams))], 1)
    rest = whole[:, 3 * FULL :]
    total = rest[:, 96:97]
    sums = [
        jnp.concatenate(
            [whole[:, n * FULL : (n + 1) * FULL], pltpu.roll(rest, (128 - 32 * n) % 128, 1)], 1
        )
        for n in range(3)
    ]
    linear = sums[0] / total
    lin_out[...] = linear
    wgt_out[...] = linear * (sums[1] * sums[1] + sums[2] * sums[2]) / (total * total)


def per_device(spectra, pair_list, mask, *, groups, halves):
    days, local, width = spectra.shape
    rows = pair_list.shape[0]
    own = rows // groups
    steps = groups.bit_length() - 1
    streams = len(streams_of(steps))
    half = PACKED // streams
    hbm = pl.BlockSpec(memory_space=pl.ANY)
    vmem = pl.BlockSpec(memory_space=pltpu.VMEM)
    lin, wgt = pl.pallas_call(
        functools.partial(kernel, groups, halves),
        out_shape=[jax.ShapeDtypeStruct((own, LANES), jnp.float32)] * 2,
        in_specs=[hbm, vmem, vmem, hbm],
        out_specs=[vmem, vmem],
        scratch_shapes=[
            pltpu.VMEM((days, local * halves, width), jnp.bfloat16),
            pltpu.VMEM((2 * F, 2 * LANES), jnp.bfloat16),
            pltpu.VMEM((2, rows, local * halves), jnp.float32),
            pltpu.VMEM((rows, PACKED), jnp.float32),
            pltpu.VMEM((3, rows, 128), jnp.float32),
            pltpu.VMEM((streams, groups, own, half), jnp.float32),
            pltpu.VMEM((streams, groups, own, half), jnp.bfloat16),
            pltpu.VMEM((streams, groups, own, half), jnp.bfloat16),
            pltpu.SemaphoreType.DMA((2,)),
            pltpu.SemaphoreType.DMA((days, halves - 1)),
            pltpu.SemaphoreType.DMA((days, halves - 1)),
            pltpu.SemaphoreType.DMA((streams, steps)),
            pltpu.SemaphoreType.DMA((streams, steps)),
        ],
        compiler_params=pltpu.CompilerParams(
            collective_id=0, has_side_effects=True, vmem_limit_bytes=48 * 1024 * 1024
        ),
    )(spectra, pair_list.T, mask, jnp.asarray(lag_table()))
    return lin[:, :LAGS].T, wgt[:, :LAGS].T


def solution(mesh):
    in_specs = (P("day", "pair", None), P("pair", None), P("day", None))
    out_specs = (P(None, ("pair", "day")), P(None, ("pair", "day")))
    return jax.shard_map(
        functools.partial(per_device, groups=mesh.shape["day"], halves=mesh.shape["pair"]),
        mesh=mesh,
        in_specs=in_specs,
        out_specs=out_specs,
        check_vma=False,
    )
```

time: 201 us -> 41.3 us (0.21)
  waiting for transfers between devices: 91 us -> 0 us
  Pallas kernels: 0 us -> 35.7 us
  blocking collectives: 33.9 us -> 0 us
  local copies, waits for them, and re-layouts: 35.1 us -> 4.65 us
  other arithmetic: 21.4 us -> 0 us
  between operations: 14.1 us -> 0.65 us
  matrix products: 4.71 us -> 0 us
    psum x1 -> x0, waiting for transfers between devices: 70.4 us -> none  [per_device(): lax.psum((lin_sum, real_sum, imag_sum, count_local), 'day')]
    pallas_call x0 -> x1, Pallas kernels: none -> 35.7 us  [per_device(): pl.pallas_call(functools.partial(kernel, groups, halves), out_shape=[jax....]
    psum x1 -> x0, blocking collectives: 33.9 us -> none  [per_device(): lax.psum((lin_sum, real_sum, imag_sum, count_local), 'day')]
    all_gather x1 -> x0, waiting for transfers between devices: 19.9 us -> none  [per_device(): gathered = lax.all_gather(spectra, 'pair', axis=1, tiled=True)]
    gather x8 -> x0, local copies, waits for them, and re-layouts: 16.5 us -> none  [the longest x4 8.23 us: one_day(): left = jnp.take(day_spec, first, axis=0).astype(jnp.float32)]
    while x43 -> x0, local copies, waits for them, and re-layouts: 14.7 us -> none
    add x4 -> x0, other arithmetic: 10.5 us -> none  [one_day(): imag_sum = imag_sum + weight[None, :] * (hilbert * inverse)]
    another operation x5 -> x0, other arithmetic: 6.04 us -> none
  transfers between devices with their start and end apart: 2 -> 0, of which waited for: 2 -> 0; matrix products, arithmetic and copies ran while one was open for 3% -> 0% of each run, Pallas kernels for 0% -> 0%
where the time goes in v1:
time: 41.3 us; the launch traced here: 41 us
  Pallas kernels  35.7 us (86%)
  local copies, waits for them, and re-layouts  4.65 us (11%)
  between operations  0.65 us (2%)
    pallas_call x1, Pallas kernels, per_device(): pl.pallas_call(functools.partial(kernel, groups, halves), out_shape=[jax....  35.7 us
    unnamed x8, local copies, waits for them, and re-layouts  4 us

profile of v1, /device:TPU:0, one launch (start us, length us, event | category | flops | bytes accessed | tf_op | source)
XLA Modules:
  0.0 41.0 jit_solution(6541596297280524559)
XLA Ops:
  0.6 0.0 copy-start
  0.6 1.6 %copy-done = bf16[1024,1024]{1,0:T(8,128)(2,1)S(1)} copy-done((bf16[1024,1024]{1,0:T(8,128)(2,1)S(1)}, bf16[1024,1024]{1,0:T(8,128)(2,1)}, u32[]{:S(2)}) %copy-start) | copy-done | bytes 2097176
  2.2 0.0 copy-start.1
  2.2 1.0 %copy-done.1 = bf16[4,64,1024]{2,1,0:T(8,128)(2,1)S(1)} copy-done((bf16[4,64,1024]{2,1,0:T(8,128)(2,1)S(1)}, bf16[4,64,1024]{2,1,0:T(8,128)(2,1)}, u32[]{:S(2)}) %copy-start.1) | copy-done | bytes 524312
  3.3 0.0 copy-start.2
  3.3 0.7 %copy-done.2 = s32[512,2]{0,1:T(2,128)S(1)} copy-done((s32[512,2]{0,1:T(2,128)S(1)}, s32[512,2]{0,1:T(2,128)}, u32[]{:S(2)}) %copy-start.2) | copy-done | bytes 4120
  4.0 0.0 copy-start.3
  4.0 0.7 %copy-done.3 = s32[4,128]{1,0:T(4,128)S(1)} copy-done((s32[4,128]{1,0:T(4,128)S(1)}, s32[4,128]{1,0:T(4,128)}, u32[]{:S(2)}) %copy-start.3) | copy-done | bytes 2072
  4.6 35.7 %shard_map.59 = (f32[32,512]{1,0:T(8,128)S(1)}, f32[32,512]{1,0:T(8,128)S(1)}) custom-call(bf16[4,64,1024]{2,1,0:T(8,128)(2,1)S(1)} %copy-done.1, s32[2,512]{1,0:T(2,128)S(1)} %bitcast.5, s32[4,128]{1,0:T(4,128)S(1)} %copy-done.3, bf16[1024,1024]{1,0:T(8,128)(2,1)S(1)} %copy-done), custom_call_target="tpu_custom_call" | custom-call | tf_op jit(solution)/shard_map/pallas_call | solution.py:221
  40.4 0.7 %slice_bitcast_fusion = (f32[401,32]{0,1:T(8,128)}, f32[401,32]{0,1:T(8,128)}) fusion(f32[32,512]{1,0:T(8,128)S(1)} %get-tuple-element.5, f32[32,512]{1,0:T(8,128)S(1)} %get-tuple-element.4), kind=kLoop, calls=%fused_computation | loop fusion | bytes 205312 | tf_op jit(solution)/shard_map/transpose | solution.py:245
Async XLA Ops:
  0.6 1.6 %copy-start = (bf16[1024,1024]{1,0:T(8,128)(2,1)S(1)}, bf16[1024,1024]{1,0:T(8,128)(2,1)}, u32[]{:S(2)}) copy-start(bf16[1024,1024]{1,0:T(8,128)(2,1)} %constant.2.clone.table) | copy-start | bytes 6291460
  2.2 1.0 %copy-start.1 = (bf16[4,64,1024]{2,1,0:T(8,128)(2,1)S(1)}, bf16[4,64,1024]{2,1,0:T(8,128)(2,1)}, u32[]{:S(2)}) copy-start(bf16[4,64,1024]{2,1,0:T(8,128)(2,1)} %spectra.1) | copy-start | bytes 1572868
  3.3 0.7 %copy-start.2 = (s32[512,2]{0,1:T(2,128)S(1)}, s32[512,2]{0,1:T(2,128)}, u32[]{:S(2)}) copy-start(s32[512,2]{0,1:T(2,128)} %param.5) | copy-start | bytes 12292
  4.0 0.7 %copy-start.3 = (s32[4,128]{1,0:T(4,128)S(1)}, s32[4,128]{1,0:T(4,128)}, u32[]{:S(2)}) copy-start(s32[4,128]{1,0:T(4,128)} %mask.1) | copy-start | bytes 6148

commit v2 on v1

v2 whole, which is shorter than its diff:
```python
import functools
import math

import jax
import jax.numpy as jnp
import ml_dtypes
import numpy as np
from jax import lax
from jax.experimental import pallas as pl
from jax.experimental.pallas import tpu as pltpu
from jax.sharding import PartitionSpec as P

F = 512
MAXLAG = 200
LAGS = 401
LANES = 512
FULL = 384
PACKED = 1280
MESH = pl.DeviceIdType.MESH
VMEM_LIMIT = 64 * 1024 * 1024


def lag_table():
    lag = np.arange(LAGS) - MAXLAG
    freq = np.arange(F)
    phase = np.mod(lag[:, None] * freq[None, :], 2 * F) * (math.pi / F)
    cosine = np.cos(phase) / math.sqrt(F)
    sine = np.sin(phase) / math.sqrt(F)
    table = np.zeros((2 * F, 2 * LANES), np.float32)
    table[:F, :LAGS] = cosine.T
    table[F:, :LAGS] = -sine.T
    table[:F, LANES : LANES + LAGS] = sine.T
    table[F:, LANES : LANES + LAGS] = cosine.T
    return table.astype(ml_dtypes.bfloat16)


def parts_of(own):
    return 2 if own % 32 == 0 else 1


def streams_of(steps, parts):
    straight = list(range(steps))
    turned = [0] + straight[2:] + [1] if steps > 2 else straight
    half = PACKED // 2
    return [(p, n * half, half, order) for p in range(parts) for n, order in enumerate((straight, turned))]


def kernel(
    groups, halves, spectra, pairs_hbm, mask_hbm, table, lin_out, wgt_out,
    spec_all, table_v, pairs, mask, pick, acc, tail, work, outbox, inbox,
    load_sem, gsend, grecv, rsend, rrecv,
):
    days, local, _ = spectra.shape
    parts, rows, _ = acc.shape
    own = rows // groups
    steps = groups.bit_length() - 1
    streams = streams_of(steps, parts)
    me = lax.axis_index("day")
    side = lax.axis_index("pair")

    def partner(bit):
        size = 1 << bit
        mine = lax.rem(lax.div(me, size), 2)
        return mine, me + (1 - 2 * mine) * size

    mine_rows = pl.ds(pl.multiple_of(side * local, local), local)
    loads = [
        pltpu.make_async_copy(pairs_hbm, pairs, load_sem.at[0]),
        pltpu.make_async_copy(mask_hbm, mask, load_sem.at[1]),
        pltpu.make_async_copy(spectra, spec_all.at[:, mine_rows, :], load_sem.at[2]),
        pltpu.make_async_copy(table, table_v, load_sem.at[3]),
    ]
    for copy in loads:
        copy.start()

    barrier = pltpu.get_barrier_semaphore()
    for off in range(1, halves):
        pl.semaphore_signal(
            barrier, inc=1, device_id=(me, lax.rem(side + off, halves)), device_id_type=MESH
        )
    for bit in range(steps):
        pl.semaphore_signal(barrier, inc=1, device_id=(partner(bit)[1], side), device_id_type=MESH)
    pl.semaphore_wait(barrier, halves - 1 + steps)

    def gather(day, off):
        return pltpu.make_async_remote_copy(
            src_ref=spectra.at[day],
            dst_ref=spec_all.at[day, mine_rows, :],
            send_sem=gsend.at[day, off - 1],
            recv_sem=grecv.at[day, off - 1],
            device_id=(me, lax.rem(side + off, halves)),
            device_id_type=MESH,
        )

    for day in range(days):
        for off in range(1, halves):
            gather(day, off).start()

    stations = local * halves
    loads[0].wait()
    loads[1].wait()
    row = lax.broadcasted_iota(jnp.int32, (stations, rows * parts), 0)
    for end in range(2):
        hot = (pairs[end : end + 1, :] == row).astype(jnp.float32).T
        hot = hot.reshape(groups, parts, own, stations)
        for part in range(parts):
            pick[end, part] = hot[:, part].reshape(rows, stations)
    acc[...] = jnp.zeros_like(acc)
    tail[...] = jnp.zeros_like(tail)
    live = mask[...].astype(jnp.float32)
    lane = lax.broadcasted_iota(jnp.int32, (rows, 128), 1)
    for part in range(parts):
        seen = [
            lax.dot_general(
                pick[end, part], live, (((1,), (1,)), ((), ())), preferred_element_type=jnp.float32
            )
            for end in range(2)
        ]
        count = jnp.sum(seen[0] * seen[1], 1, keepdims=True)
        tail[0, part] = jnp.where(lane == 96, count, 0.0)
    loads[2].wait()
    loads[3].wait()

    block = min(rows, 256)

    def arrive(day):
        for off in range(1, halves):
            gather(day, off).wait()

    def correlate(day, part):
        today = mask[pl.ds(day, 1), :].astype(jnp.float32)
        spec = spec_all[day]
        for start in range(0, rows, block):
            here = pl.ds(start, block)
            left, right = (
                jnp.dot(
                    (pick[end, part, here] * today).astype(jnp.bfloat16),
                    spec,
                    preferred_element_type=jnp.float32,
                )
                for end in range(2)
            )
            left_re, left_im = left[:, :F], left[:, F:]
            right_re, right_im = right[:, :F], right[:, F:]
            cross = jnp.concatenate(
                [
                    (left_re * right_re + left_im * right_im).astype(jnp.bfloat16),
                    (left_im * right_re - left_re * right_im).astype(jnp.bfloat16),
                ],
                1,
            )
            analytic = jnp.dot(cross, table_v[...], preferred_element_type=jnp.float32)
            trace, hilbert = analytic[:, :LANES], analytic[:, LANES:]
            inverse = lax.rsqrt(jnp.maximum(trace * trace + hilbert * hilbert, 0.25))
            for n, value in enumerate((trace, trace * inverse, hilbert * inverse)):
                acc[part, here, n * FULL : (n + 1) * FULL] += value[:, :FULL]
                tail[n, part, here] += value[:, FULL:]

    def exchange(s, k):
        blocks = groups >> (k + 1)
        base = groups - (groups >> k)
        return pltpu.make_async_remote_copy(
            src_ref=outbox.at[s, pl.ds(base, blocks)],
            dst_ref=inbox.at[s, pl.ds(base, blocks)],
            send_sem=rsend.at[s, k],
            recv_sem=rrecv.at[s, k],
            device_id=(partner(streams[s][3][k])[1], side),
            device_id_type=MESH,
        )

    def first_rows(order, i, bit):
        natural = sum(((i >> (steps - 1 - n)) & 1) << order[n] for n in range(1, steps))
        return pl.ds(pl.multiple_of((natural + bit) * own, own), own)

    def send(s, k):
        part, lane0, width, order = streams[s]
        theirs = 1 - partner(order[k])[0]
        blocks = groups >> (k + 1)
        base = groups - (groups >> k)
        before = groups - (groups >> (k - 1)) if k else 0
        for i in range(blocks):
            if k == 0:
                sent = acc[part, first_rows(order, i, theirs), pl.ds(lane0, width)]
            else:
                sent = work[s, before + theirs * blocks + i]
            outbox[s, base + i] = sent.astype(jnp.bfloat16)
        exchange(s, k).start()

    def receive(s, k):
        part, lane0, width, order = streams[s]
        mine = partner(order[k])[0]
        blocks = groups >> (k + 1)
        base = groups - (groups >> k)
        before = groups - (groups >> (k - 1)) if k else 0
        exchange(s, k).wait_recv()
        for i in range(blocks):
            if k == 0:
                kept = acc[part, first_rows(order, i, mine), pl.ds(lane0, width)]
            else:
                kept = work[s, before + mine * blocks + i]
            work[s, base + i] = kept + inbox[s, base + i].astype(jnp.float32)

    def one_day(day, carry):
        arrive(day)
        for part in range(parts):
            correlate(day, part)
        return carry

    lax.fori_loop(0, days - 1, one_day, 0)
    arrive(days - 1)
    for part in range(parts):
        correlate(days - 1, part)
        acc[part, :, 3 * FULL :] = (
            tail[0, part] + pltpu.roll(tail[1, part], 32, 1) + pltpu.roll(tail[2, part], 64, 1)
        )
        for s in range(len(streams)):
            if streams[s][0] == part:
                send(s, 0)
    for k in range(steps):
        for s in range(len(streams)):
            receive(s, k)
            if k + 1 < steps:
                send(s, k + 1)

    last = groups - 2
    for part in range(parts):
        whole = jnp.concatenate([work[s, last] for s in range(len(streams)) if streams[s][0] == part], 1)
        rest = whole[:, 3 * FULL :]
        total = rest[:, 96:97]
        sums = [
            jnp.concatenate(
                [whole[:, n * FULL : (n + 1) * FULL], pltpu.roll(rest, (128 - 32 * n) % 128, 1)], 1
            )
            for n in range(3)
        ]
        linear = sums[0] / total
        here = pl.ds(part * own, own)
        lin_out[here] = linear
        wgt_out[here] = linear * (sums[1] * sums[1] + sums[2] * sums[2]) / (total * total)
    for s in range(len(streams)):
        for k in range(steps):
            exchange(s, k).wait_send()


def per_device(spectra, pair_list, mask, *, groups, halves):
    days, local, width = spectra.shape
    rows = pair_list.shape[0]
    parts = parts_of(rows // groups)
    own = rows // groups // parts
    steps = groups.bit_length() - 1
    streams = len(streams_of(steps, parts))
    half = PACKED // 2
    hbm = pl.BlockSpec(memory_space=pl.ANY)
    vmem = pl.BlockSpec(memory_space=pltpu.VMEM)
    lin, wgt = pl.pallas_call(
        functools.partial(kernel, groups, halves),
        out_shape=[jax.ShapeDtypeStruct((own * parts, LANES), jnp.float32)] * 2,
        in_specs=[hbm] * 4,
        out_specs=[vmem, vmem],
        scratch_shapes=[
            pltpu.VMEM((days, local * halves, width), jnp.bfloat16),
            pltpu.VMEM((2 * F, 2 * LANES), jnp.bfloat16),
            pltpu.VMEM((2, rows), jnp.int32),
            pltpu.VMEM(mask.shape, jnp.int32),
            pltpu.VMEM((2, parts, rows // parts, local * halves), jnp.float32),
            pltpu.VMEM((parts, rows // parts, PACKED), jnp.float32),
            pltpu.VMEM((3, parts, rows // parts, 128), jnp.float32),
            pltpu.VMEM((streams, groups, own, half), jnp.float32),
            pltpu.VMEM((streams, groups, own, half), jnp.bfloat16),
            pltpu.VMEM((streams, groups, own, half), jnp.bfloat16),
            pltpu.SemaphoreType.DMA((4,)),
            pltpu.SemaphoreType.DMA((days, halves - 1)),
            pltpu.SemaphoreType.DMA((days, halves - 1)),
            pltpu.SemaphoreType.DMA((streams, steps)),
            pltpu.SemaphoreType.DMA((streams, steps)),
        ],
        compiler_params=pltpu.CompilerParams(
            collective_id=0, has_side_effects=True, vmem_limit_bytes=VMEM_LIMIT
        ),
    )(spectra, pair_list.T, mask, jnp.asarray(lag_table()))
    return lin[:, :LAGS].T, wgt[:, :LAGS].T


def solution(mesh):
    in_specs = (P("day", "pair", None), P("pair", None), P("day", None))
    out_specs = (P(None, ("pair", "day")), P(None, ("pair", "day")))
    return jax.shard_map(
        functools.partial(per_device, groups=mesh.shape["day"], halves=mesh.shape["pair"]),
        mesh=mesh,
        in_specs=in_specs,
        out_specs=out_specs,
        check_vma=False,
    )
```

time: 41.3 us -> 37.5 us (0.908)
  local copies, waits for them, and re-layouts: 4.65 us -> 1.53 us
  Pallas kernels: 35.7 us -> 35.2 us
    unnamed x8 -> x0, local copies, waits for them, and re-layouts: 4 us -> none
    transpose x1, local copies, waits for them, and re-layouts: 0.66 us -> 1.53 us  [per_device(): return (lin[:, :LAGS].T, wgt[:, :LAGS].T)]
    pallas_call x1, Pallas kernels: 35.7 us -> 35.2 us  [per_device(): pl.pallas_call(functools.partial(kernel, groups, halves), out_shape=[jax....]
where the time goes in v2:
time: 37.5 us; the launch traced here: 37.4 us
  Pallas kernels  35.2 us (94%)
  local copies, waits for them, and re-layouts  1.53 us (4%)
  between operations  0.64 us (2%)
    pallas_call x1, Pallas kernels, per_device(): pl.pallas_call(functools.partial(kernel, groups, halves), out_shape=[jax....  35.2 us
    transpose x1, local copies, waits for them, and re-layouts, per_device(): return (lin[:, :LAGS].T, wgt[:, :LAGS].T)  1.53 us

profile of v2, /device:TPU:0, one launch (start us, length us, event | category | flops | bytes accessed | tf_op | source)
XLA Modules:
  0.0 37.4 jit_solution(14935202215719247260)
XLA Ops:
  0.6 35.2 %shard_map.59 = (f32[32,512]{1,0:T(8,128)}, f32[32,512]{1,0:T(8,128)}) custom-call(bf16[4,64,1024]{2,1,0:T(8,128)(2,1)} %spectra.1, s32[2,512]{1,0:T(2,128)} %bitcast.5, s32[4,128]{1,0:T(4,128)} %mask_hbm.1, bf16[1024,1024]{1,0:T(8,128)(2,1)} %constant.2.clone.table), custom_call_target="tpu_custom_call" | custom-call | tf_op jit(solution)/shard_map/pallas_call | solution.py:255
  35.8 1.5 %slice_bitcast_fusion = (f32[401,32]{0,1:T(8,128)}, f32[401,32]{0,1:T(8,128)}) fusion(f32[32,512]{1,0:T(8,128)} %get-tuple-element.5, f32[32,512]{1,0:T(8,128)} %get-tuple-element.4), kind=kLoop, calls=%fused_computation | loop fusion | bytes 205312 | tf_op jit(solution)/shard_map/transpose | solution.py:281

commit v3 on v2

v3 whole, which is shorter than its diff:
```python
import functools
import math

import jax
import jax.numpy as jnp
import ml_dtypes
import numpy as np
from jax import lax
from jax.experimental import pallas as pl
from jax.experimental.pallas import tpu as pltpu
from jax.sharding import PartitionSpec as P

F = 512
MAXLAG = 200
LAGS = 401
LANES = 512
FULL = 384
PACKED = 1280
MESH = pl.DeviceIdType.MESH
VMEM_LIMIT = 40 * 1024 * 1024


def lag_table():
    lag = np.arange(LAGS) - MAXLAG
    freq = np.arange(F)
    phase = np.mod(lag[:, None] * freq[None, :], 2 * F) * (math.pi / F)
    cosine = np.cos(phase) / math.sqrt(F)
    sine = np.sin(phase) / math.sqrt(F)
    table = np.zeros((2 * F, 2 * LANES), np.float32)
    table[:F, :LAGS] = cosine.T
    table[F:, :LAGS] = -sine.T
    table[:F, LANES : LANES + LAGS] = sine.T
    table[F:, LANES : LANES + LAGS] = cosine.T
    return table.astype(ml_dtypes.bfloat16)


def parts_of(own):
    return 2 if own % 32 == 0 else 1


def parts_of(own):
    return 2 if own % 32 == 0 else 1


def streams_of(steps, parts):
    straight = list(range(steps))
    half = PACKED // 2
    return [
        (p, n * half, half, order)
        for p in range(parts)
        for n, order in enumerate((straight, straight[1:] + straight[:1]))
    ]


def kernel(
    chips, halves, spectra, pairs_hbm, mask_hbm, table, lin_out, wgt_out,
    spec_all, table_v, pairs, mask, hot, pick, acc, tail, work, outbox, inbox,
    load_sem, gsend, grecv, fsend, frecv, dsend, drecv, rsend, rrecv,
):
    days, local, _ = spectra.shape
    rows = acc.shape[0]
    steps = chips.bit_length() - 1
    parts = parts_of(rows // chips)
    per_part = rows // parts
    own = per_part // chips
    streams = streams_of(steps, parts)
    me = lax.axis_index("day")
    side = lax.axis_index("pair")
    core = lax.rem(me, 2)
    sibling = me + 1 - 2 * core

    def partner(bit):
        size = 2 << bit
        mine = lax.rem(lax.div(me, size), 2)
        return mine, me + (1 - 2 * mine) * size

    def stations_of(where):
        return pl.ds(pl.multiple_of(where * local, local), local)

    mine_rows = stations_of(side)
    loads = [
        pltpu.make_async_copy(pairs_hbm, pairs, load_sem.at[0]),
        pltpu.make_async_copy(mask_hbm, mask.at[core], load_sem.at[1]),
        pltpu.make_async_copy(spectra, spec_all.at[core, :, mine_rows, :], load_sem.at[2]),
        pltpu.make_async_copy(table, table_v, load_sem.at[3]),
    ]
    for copy in loads:
        copy.start()

    barrier = pltpu.get_barrier_semaphore()
    for off in range(1, halves):
        pl.semaphore_signal(
            barrier, inc=1, device_id=(me, lax.rem(side + off, halves)), device_id_type=MESH
        )
    pl.semaphore_signal(barrier, inc=1, device_id=(sibling, side), device_id_type=MESH)
    for bit in range(steps):
        pl.semaphore_signal(barrier, inc=1, device_id=(partner(bit)[1], side), device_id_type=MESH)
    pl.semaphore_wait(barrier, halves + steps)

    def gather(day, off):
        return pltpu.make_async_remote_copy(
            src_ref=spectra.at[day],
            dst_ref=spec_all.at[core, day, mine_rows, :],
            send_sem=gsend.at[day, off - 1],
            recv_sem=grecv.at[day, off - 1],
            device_id=(me, lax.rem(side + off, halves)),
            device_id_type=MESH,
        )

    def forward(day, off):
        here = spec_all.at[core, day, stations_of(lax.rem(side + halves - off, halves)), :]
        return pltpu.make_async_remote_copy(
            src_ref=here,
            dst_ref=here,
            send_sem=fsend.at[day, off - 1],
            recv_sem=frecv.at[day, off - 1],
            device_id=(sibling, side),
            device_id_type=MESH,
        )

    def direct(day):
        return pltpu.make_async_remote_copy(
            src_ref=spectra.at[day],
            dst_ref=spec_all.at[core, day, mine_rows, :],
            send_sem=dsend.at[day],
            recv_sem=drecv.at[day],
            device_id=(sibling, side),
            device_id_type=MESH,
        )

    mask_copy = pltpu.make_async_remote_copy(
        src_ref=mask_hbm,
        dst_ref=mask.at[core],
        send_sem=dsend.at[days],
        recv_sem=drecv.at[days],
        device_id=(sibling, side),
        device_id_type=MESH,
    )

    for day in range(days):
        for off in range(1, halves):
            gather(day, off).start()
        if day == 0:
            mask_copy.start()
        direct(day).start()

    stations = local * halves
    loads[0].wait()
    for end in range(2):
        row = lax.broadcasted_iota(jnp.int32, (stations, 2 * rows), 0)
        hot[...] = (pairs[end : end + 1, :] == row).astype(jnp.float32).T
        for part in range(parts):
            for chip in range(chips):
                first = (2 * chip + core) * (own * parts) + part * own
                pick[end, pl.ds(part * per_part + chip * own, own)] = hot[
                    pl.ds(pl.multiple_of(first, own), own)
                ]
    acc[...] = jnp.zeros_like(acc)
    tail[...] = jnp.zeros_like(tail)
    loads[1].wait()
    mask_copy.wait_recv()
    count = 0.0
    for owner in range(2):
        seen = [
            lax.dot_general(
                pick[end],
                mask[owner].astype(jnp.float32),
                (((1,), (1,)), ((), ())),
                preferred_element_type=jnp.float32,
            )
            for end in range(2)
        ]
        count += jnp.sum(seen[0] * seen[1], 1, keepdims=True)
    lane = lax.broadcasted_iota(jnp.int32, (rows, 128), 1)
    tail[0] = jnp.where(lane == 96, count, 0.0)
    loads[2].wait()
    loads[3].wait()

    def correlate(owner, day, start, size):
        today = mask[owner, pl.ds(day, 1), :].astype(jnp.float32)
        spec = spec_all[owner, day]
        here = pl.ds(start, size)
        left, right = (
            jnp.dot(
                (pick[end, here] * today).astype(jnp.bfloat16),
                spec,
                preferred_element_type=jnp.float32,
            )
            for end in range(2)
        )
        left_re, left_im = left[:, :F], left[:, F:]
        right_re, right_im = right[:, :F], right[:, F:]
        cross = jnp.concatenate(
            [
                (left_re * right_re + left_im * right_im).astype(jnp.bfloat16),
                (left_im * right_re - left_re * right_im).astype(jnp.bfloat16),
            ],
            1,
        )
        analytic = jnp.dot(cross, table_v[...], preferred_element_type=jnp.float32)
        trace, hilbert = analytic[:, :LANES], analytic[:, LANES:]
        inverse = lax.rsqrt(jnp.maximum(trace * trace + hilbert * hilbert, 0.25))
        for n, value in enumerate((trace, trace * inverse, hilbert * inverse)):
            acc[here, n * FULL : (n + 1) * FULL] += value[:, :FULL]
            tail[n, here] += value[:, FULL:]

    def exchange(s, k):
        blocks = chips >> (k + 1)
        base = chips - (chips >> k)
        return pltpu.make_async_remote_copy(
            src_ref=outbox.at[s, pl.ds(base, blocks)],
            dst_ref=inbox.at[s, pl.ds(base, blocks)],
            send_sem=rsend.at[s, k],
            recv_sem=rrecv.at[s, k],
            device_id=(partner(streams[s][3][k])[1], side),
            device_id_type=MESH,
        )

    def first_rows(part, order, i, bit):
        natural = sum(((i >> (steps - 1 - n)) & 1) << order[n] for n in range(1, steps))
        first = part * per_part + (natural + bit * (1 << order[0])) * own
        return pl.ds(pl.multiple_of(first, own), own)

    def send(s, k):
        part, lane0, width, order = streams[s]
        theirs = 1 - partner(order[k])[0]
        blocks = chips >> (k + 1)
        base = chips - (chips >> k)
        before = chips - (chips >> (k - 1)) if k else 0
        for i in range(blocks):
            if k == 0:
                sent = acc[first_rows(part, order, i, theirs), pl.ds(lane0, width)]
            else:
                sent = work[s, before + theirs * blocks + i]
            outbox[s, base + i] = sent.astype(jnp.bfloat16)
        exchange(s, k).start()

    def receive(s, k):
        part, lane0, width, order = streams[s]
        mine = partner(order[k])[0]
        blocks = chips >> (k + 1)
        base = chips - (chips >> k)
        before = chips - (chips >> (k - 1)) if k else 0
        exchange(s, k).wait_recv()
        for i in range(blocks):
            if k == 0:
                kept = acc[first_rows(part, order, i, mine), pl.ds(lane0, width)]
            else:
                kept = work[s, before + mine * blocks + i]
            work[s, base + i] = kept + inbox[s, base + i].astype(jnp.float32)

    def own_day(day):
        for off in range(1, halves):
            gather(day, off).wait_recv()
            forward(day, off).start()
        correlate(core, day, 0, rows)
        direct(day).wait_recv()
        for off in range(1, halves):
            forward(day, off).wait_recv()

    def one_day(day, carry):
        own_day(day)
        correlate(1 - core, day, 0, rows)
        return carry

    lax.fori_loop(0, days - 1, one_day, 0)
    own_day(days - 1)
    for part in range(parts):
        here = pl.ds(part * per_part, per_part)
        correlate(1 - core, days - 1, part * per_part, per_part)
        acc[here, 3 * FULL :] = (
            tail[0, here] + pltpu.roll(tail[1, here], 32, 1) + pltpu.roll(tail[2, here], 64, 1)
        )
        for s in range(len(streams)):
            if streams[s][0] == part:
                send(s, 0)
    for k in range(steps):
        for s in range(len(streams)):
            receive(s, k)
            if k + 1 < steps:
                send(s, k + 1)

    last = chips - 2
    for part in range(parts):
        whole = jnp.concatenate(
            [work[s, last] for s in range(len(streams)) if streams[s][0] == part], 1
        )
        rest = whole[:, 3 * FULL :]
        total = rest[:, 96:97]
        sums = [
            jnp.concatenate(
                [whole[:, n * FULL : (n + 1) * FULL], pltpu.roll(rest, (128 - 32 * n) % 128, 1)], 1
            )
            for n in range(3)
        ]
        linear = sums[0] / total
        here = pl.ds(part * own, own)
        lin_out[here] = linear
        wgt_out[here] = linear * (sums[1] * sums[1] + sums[2] * sums[2]) / (total * total)
    mask_copy.wait_send()
    for day in range(days):
        direct(day).wait_send()
        for off in range(1, halves):
            gather(day, off).wait_send()
            forward(day, off).wait_send()
    for s in range(len(streams)):
        for k in range(steps):
            exchange(s, k).wait_send()


def per_device(spectra, pair_list, mask, *, groups, halves):
    days, local, width = spectra.shape
    chips = groups // 2
    rows = pair_list.shape[0] // 2
    parts = parts_of(rows // chips)
    own = rows // chips // parts
    steps = chips.bit_length() - 1
    streams = len(streams_of(steps, parts))
    half = PACKED // 2
    stations = local * halves
    operands = (spectra, pair_list.T, mask, jnp.asarray(lag_table()))
    hbm = pl.BlockSpec(memory_space=pltpu.HBM)
    vmem = pl.BlockSpec(memory_space=pltpu.VMEM)
    lin, wgt = pl.pallas_call(
        functools.partial(kernel, chips, halves),
        out_shape=[jax.ShapeDtypeStruct((own * parts, LANES), jnp.float32)] * 2,
        in_specs=[hbm] * 4,
        out_specs=[vmem, vmem],
        scratch_shapes=[
            pltpu.VMEM((2, days, stations, width), jnp.bfloat16),
            pltpu.VMEM((2 * F, 2 * LANES), jnp.bfloat16),
            pltpu.VMEM((2, 2 * rows), jnp.int32),
            pltpu.VMEM((2, *mask.shape), jnp.int32),
            pltpu.VMEM((2 * rows, stations), jnp.float32),
            pltpu.VMEM((2, rows, stations), jnp.float32),
            pltpu.VMEM((rows, PACKED), jnp.float32),
            pltpu.VMEM((3, rows, 128), jnp.float32),
            pltpu.VMEM((streams, chips, own, half), jnp.float32),
            pltpu.VMEM((streams, chips, own, half), jnp.bfloat16),
            pltpu.VMEM((streams, chips, own, half), jnp.bfloat16),
            pltpu.SemaphoreType.DMA((4,)),
            pltpu.SemaphoreType.DMA((days, halves - 1)),
            pltpu.SemaphoreType.DMA((days, halves - 1)),
            pltpu.SemaphoreType.DMA((days, halves - 1)),
            pltpu.SemaphoreType.DMA((days, halves - 1)),
            pltpu.SemaphoreType.DMA((days + 1,)),
            pltpu.SemaphoreType.DMA((days + 1,)),
            pltpu.SemaphoreType.DMA((streams, steps)),
            pltpu.SemaphoreType.DMA((streams, steps)),
        ],
        compiler_params=pltpu.CompilerParams(
            collective_id=0, has_side_effects=True, vmem_limit_bytes=VMEM_LIMIT
        ),
    )(*[pltpu.with_memory_space_constraint(x, pltpu.HBM) for x in operands])
    return lin[:, :LAGS].T, wgt[:, :LAGS].T


def solution(mesh):
    in_specs = (P("day", "pair", None), P("pair", None), P("day", None))
    out_specs = (P(None, ("pair", "day")), P(None, ("pair", "day")))
    return jax.shard_map(
        functools.partial(per_device, groups=mesh.shape["day"], halves=mesh.shape["pair"]),
        mesh=mesh,
        in_specs=in_specs,
        out_specs=out_specs,
        check_vma=False,
    )
```

time: 37.5 us -> 35.4 us (0.944)
  Pallas kernels: 35.2 us -> 33.9 us
  local copies, waits for them, and re-layouts: 1.53 us -> 0.66 us
    pallas_call x1, Pallas kernels: 35.2 us -> 33.9 us  [per_device(): pl.pallas_call(functools.partial(kernel, chips, halves), out_shape=[jax.S...]
    transpose x1, local copies, waits for them, and re-layouts: 1.53 us -> 0.66 us  [per_device(): return (lin[:, :LAGS].T, wgt[:, :LAGS].T)]
where the time goes in v3:
time: 35.4 us; the launch traced here: 35.2 us
  Pallas kernels  33.9 us (96%)
  local copies, waits for them, and re-layouts  0.66 us (2%)
  between operations  0.64 us (2%)
    pallas_call x1, Pallas kernels, per_device(): pl.pallas_call(functools.partial(kernel, chips, halves), out_shape=[jax.S...  33.9 us

profile of v3, /device:TPU:0, one launch (start us, length us, event | category | flops | bytes accessed | tf_op | source)
XLA Modules:
  0.0 35.2 jit_solution(6766484948636749183)
XLA Ops:
  0.6 33.9 %shard_map.59 = (f32[32,512]{1,0:T(8,128)S(1)}, f32[32,512]{1,0:T(8,128)S(1)}) custom-call(bf16[4,64,1024]{2,1,0:T(8,128)(2,1)} %spectra.1, s32[2,512]{1,0:T(2,128)} %bitcast.5, s32[4,128]{1,0:T(4,128)} %mask_hbm.1, bf16[1024,1024]{1,0:T(8,128)(2,1)} %constant.2.clone.table), custom_call_target="tpu_custom_call" | custom-call | tf_op jit(solution)/shard_map/pallas_call | solution.py:324
  34.6 0.7 %slice_bitcast_fusion = (f32[401,32]{0,1:T(8,128)}, f32[401,32]{0,1:T(8,128)}) fusion(f32[32,512]{1,0:T(8,128)S(1)} %get-tuple-element.5, f32[32,512]{1,0:T(8,128)S(1)} %get-tuple-element.4), kind=kLoop, calls=%fused_computation | loop fusion | bytes 205312 | tf_op jit(solution)/shard_map/transpose | solution.py:355

commit v4 on v3

--- a/solution.py
+++ b/solution.py
@@ -14,24 +14,67 @@
 MAXLAG = 200
 LAGS = 401
 LANES = 512
-FULL = 384
+WIDE = 256
 PACKED = 1280
+SHARES = (896, 384)
 MESH = pl.DeviceIdType.MESH
 VMEM_LIMIT = 40 * 1024 * 1024
 
 
 def lag_table():
-    lag = np.arange(LAGS) - MAXLAG
+    lag = np.arange(MAXLAG + 1)
     freq = np.arange(F)
-    phase = np.mod(lag[:, None] * freq[None, :], 2 * F) * (math.pi / F)
-    cosine = np.cos(phase) / math.sqrt(F)
-    sine = np.sin(phase) / math.sqrt(F)
-    table = np.zeros((2 * F, 2 * LANES), np.float32)
-    table[:F, :LAGS] = cosine.T
-    table[F:, :LAGS] = -sine.T
-    table[:F, LANES : LANES + LAGS] = sine.T
-    table[F:, LANES : LANES + LAGS] = cosine.T
+    phase = np.mod(lag[None, :] * freq[:, None], 2 * F) * (math.pi / F)
+    table = np.zeros((F, 2 * WIDE), np.float32)
+    table[:, : MAXLAG + 1] = np.cos(phase) / math.sqrt(F)
+    table[:, WIDE : WIDE + MAXLAG + 1] = np.sin(phase) / math.sqrt(F)
     return table.astype(ml_dtypes.bfloat16)
+
+
+def packed_rest(tail, count):
+    lane = lax.broadcasted_iota(jnp.int32, count.shape, 1)
+    tiles = [
+        jnp.where(lane < 64, tail[2 * n], pltpu.roll(tail[2 * n + 1], 64, 1)) for n in range(3)
+    ]
+    ends = count
+    for j in range(6):
+        ends += pltpu.roll(jnp.where(lane >= 64, tail[j], 0.0), (16 * j + 64) % 128, 1)
+    return jnp.concatenate(tiles + [ends], 1)
+
+
+def unpacked(whole):
+    tile = [whole[:, n * 128 : (n + 1) * 128] for n in range(PACKED // 128)]
+    lane = lax.broadcasted_iota(jnp.int32, tile[0].shape, 1)
+    sums = []
+    for j in range(6):
+        middle = tile[6 + j // 2] if j % 2 == 0 else pltpu.roll(tile[6 + j // 2], 64, 1)
+        end = pltpu.roll(tile[9], (192 - 16 * j) % 128, 1)
+        rest = jnp.where(lane < 64, middle, jnp.where(lane < 73, end, 0.0))
+        sums.append(jnp.concatenate([tile[j], rest], 1))
+    return sums, tile[9][:, 96:97]
+
+
+def in_order(plus, minus, turn):
+    rows = minus.shape[0]
+    high = minus.astype(jnp.bfloat16)
+    left = minus - high.astype(jnp.float32)
+    middle = left.astype(jnp.bfloat16)
+    low = (left - middle.astype(jnp.float32)).astype(jnp.bfloat16)
+    terms = jnp.dot(
+        jnp.concatenate([high, middle, low], 0), turn, preferred_element_type=jnp.float32
+    )
+    turned = terms[:rows] + terms[rows : 2 * rows] + terms[2 * rows :]
+    near, far = (pltpu.roll(plus[:, n * 128 : (n + 1) * 128], 72, 1) for n in range(2))
+    lane = lax.broadcasted_iota(jnp.int32, near.shape, 1)
+    return jnp.concatenate(
+        [
+            turned[:, :128],
+            jnp.where(lane < 72, turned[:, 128:], near),
+            jnp.where(lane < 72, near, far),
+            far,
+        ],
+        1,
+    )
 
 
 def parts_of(own):
@@ -44,19 +87,20 @@
 
 def streams_of(steps, parts):
     straight = list(range(steps))
-    half = PACKED // 2
+    swapped = straight[1::-1] + straight[2:]
     return [
-        (p, n * half, half, order)
+        (p, n, n * SHARES[0], SHARES[n], order)
         for p in range(parts)
-        for n, order in enumerate((straight, straight[1:] + straight[:1]))
+        for n, order in enumerate((straight, swapped))
     ]
 
 
 def kernel(
     chips, halves, spectra, pairs_hbm, mask_hbm, table, lin_out, wgt_out,
-    spec_all, table_v, pairs, mask, hot, pick, acc, tail, work, outbox, inbox,
-    load_sem, gsend, grecv, fsend, frecv, dsend, drecv, rsend, rrecv,
+    spec_all, table_v, pairs, mask, hot, pick, acc, tail, count, turn, *boxes_and_semaphores,
 ):
+    work, outbox, inbox = (boxes_and_semaphores[2 * n : 2 * n + 2] for n in range(3))
+    load_sem, gsend, grecv, fsend, frecv, dsend, drecv, rsend, rrecv = boxes_and_semaphores[6:]
     days, local, _ = spectra.shape
     rows = acc.shape[0]
     steps = chips.bit_length() - 1
@@ -159,7 +203,7 @@
     tail[...] = jnp.zeros_like(tail)
     loads[1].wait()
     mask_copy.wait_recv()
-    count = 0.0
+    alive = 0.0
     for owner in range(2):
         seen = [
             lax.dot_general(
@@ -170,9 +214,18 @@
             )
             for end in range(2)
         ]
-        count += jnp.sum(seen[0] * seen[1], 1, keepdims=True)
+        alive += jnp.sum(seen[0] * seen[1], 1, keepdims=True)
     lane = lax.broadcasted_iota(jnp.int32, (rows, 128), 1)
-    tail[0] = jnp.where(lane == 96, count, 0.0)
+    count[...] = jnp.where(lane == 96, alive, 0.0)
+    turn[...] = (
+        (
+            lax.broadcasted_iota(jnp.int32, (WIDE, WIDE), 0)
+            + lax.broadcasted_iota(jnp.int32, (WIDE, WIDE), 1)
+            == MAXLAG
+        )
+        .astype(jnp.float32)
+        .astype(jnp.bfloat16)
+    )
     loads[2].wait()
     loads[3].wait()
 
@@ -180,39 +233,44 @@
         today = mask[owner, pl.ds(day, 1), :].astype(jnp.float32)
         spec = spec_all[owner, day]
         here = pl.ds(start, size)
-        left, right = (
-            jnp.dot(
-                (pick[end, here] * today).astype(jnp.bfloat16),
-                spec,
-                preferred_element_type=jnp.float32,
-            )
-            for end in range(2)
-        )
-        left_re, left_im = left[:, :F], left[:, F:]
-        right_re, right_im = right[:, :F], right[:, F:]
+        both = jnp.dot(
+            (pick[:, here] * today).astype(jnp.bfloat16).reshape(2 * size, spec.shape[0]),
+            spec,
+            preferred_element_type=jnp.float32,
+        )
+        left_re, left_im = both[:size, :F], both[:size, F:]
+        right_re, right_im = both[size:, :F], both[size:, F:]
         cross = jnp.concatenate(
             [
                 (left_re * right_re + left_im * right_im).astype(jnp.bfloat16),
                 (left_im * right_re - left_re * right_im).astype(jnp.bfloat16),
             ],
-            1,
-        )
-        analytic = jnp.dot(cross, table_v[...], preferred_element_type=jnp.float32)
-        trace, hilbert = analytic[:, :LANES], analytic[:, LANES:]
-        inverse = lax.rsqrt(jnp.maximum(trace * trace + hilbert * hilbert, 0.25))
-        for n, value in enumerate((trace, trace * inverse, hilbert * inverse)):
-            acc[here, n * FULL : (n + 1) * FULL] += value[:, :FULL]
-            tail[n, here] += value[:, FULL:]
+            0,
+        )
+        waves = jnp.dot(cross, table_v[...], preferred_element_type=jnp.float32)
+        re_cos, re_sin = waves[:size, :WIDE], waves[:size, WIDE:]
+        im_cos, im_sin = waves[size:, :WIDE], waves[size:, WIDE:]
+        for back in range(2):
+            if back:
+                trace, hilbert = re_cos + im_sin, im_cos - re_sin
+            else:
+                trace, hilbert = re_cos - im_sin, im_cos + re_sin
+            inverse = lax.rsqrt(jnp.maximum(trace * trace + hilbert * hilbert, 0.25))
+            for n, value in enumerate((trace, trace * inverse, hilbert * inverse)):
+                j = 2 * n + back
+                acc[here, j * 128 : (j + 1) * 128] += value[:, :128]
+                tail[j, here] += value[:, 128:]
 
     def exchange(s, k):
+        part, n, _, _, order = streams[s]
         blocks = chips >> (k + 1)
         base = chips - (chips >> k)
         return pltpu.make_async_remote_copy(
-            src_ref=outbox.at[s, pl.ds(base, blocks)],
-            dst_ref=inbox.at[s, pl.ds(base, blocks)],
+            src_ref=outbox[n].at[part, pl.ds(base, blocks)],
+            dst_ref=inbox[n].at[part, pl.ds(base, blocks)],
             send_sem=rsend.at[s, k],
             recv_sem=rrecv.at[s, k],
-            device_id=(partner(streams[s][3][k])[1], side),
+            device_id=(partner(order[k])[1], side),
             device_id_type=MESH,
         )
 
@@ -222,7 +280,7 @@
         return pl.ds(pl.multiple_of(first, own), own)
 
     def send(s, k):
-        part, lane0, width, order = streams[s]
+        part, n, lane0, width, order = streams[s]
         theirs = 1 - partner(order[k])[0]
         blocks = chips >> (k + 1)
         base = chips - (chips >> k)
@@ -231,12 +289,12 @@
             if k == 0:
                 sent = acc[first_rows(part, order, i, theirs), pl.ds(lane0, width)]
             else:
-                sent = work[s, before + theirs * blocks + i]
-            outbox[s, base + i] = sent.astype(jnp.bfloat16)
+                sent = work[n][part, before + theirs * blocks + i]
+            outbox[n][part, base + i] = sent.astype(jnp.bfloat16)
         exchange(s, k).start()
 
     def receive(s, k):
-        part, lane0, width, order = streams[s]
+        part, n, lane0, width, order = streams[s]
         mine = partner(order[k])[0]
         blocks = chips >> (k + 1)
         base = chips - (chips >> k)
@@ -246,8 +304,8 @@
             if k == 0:
                 kept = acc[first_rows(part, order, i, mine), pl.ds(lane0, width)]
             else:
-                kept = work[s, before + mine * blocks + i]
-            work[s, base + i] = kept + inbox[s, base + i].astype(jnp.float32)
+                kept = work[n][part, before + mine * blocks + i]
+            work[n][part, base + i] = kept + inbox[n][part, base + i].astype(jnp.float32)
 
     def own_day(day):
         for off in range(1, halves):
@@ -268,9 +326,7 @@
     for part in range(parts):
         here = pl.ds(part * per_part, per_part)
         correlate(1 - core, days - 1, part * per_part, per_part)
-        acc[here, 3 * FULL :] = (
-            tail[0, here] + pltpu.roll(tail[1, here], 32, 1) + pltpu.roll(tail[2, here], 64, 1)
-        )
+        acc[here, 6 * 128 :] = packed_rest([tail[j, here] for j in range(6)], count[here])
         for s in range(len(streams)):
             if streams[s][0] == part:
                 send(s, 0)
@@ -281,22 +337,26 @@
                 send(s, k + 1)
 
     last = chips - 2
-    for part in range(parts):
-        whole = jnp.concatenate(
-            [work[s, last] for s in range(len(streams)) if streams[s][0] == part], 1
-        )
-        rest = whole[:, 3 * FULL :]
-        total = rest[:, 96:97]
-        sums = [
-            jnp.concatenate(
-                [whole[:, n * FULL : (n + 1) * FULL], pltpu.roll(rest, (128 - 32 * n) % 128, 1)], 1
-            )
-            for n in range(3)
-        ]
-        linear = sums[0] / total
-        here = pl.ds(part * own, own)
-        lin_out[here] = linear
-        wgt_out[here] = linear * (sums[1] * sums[1] + sums[2] * sums[2]) / (total * total)
+    whole = jnp.concatenate(
+        [
+            jnp.concatenate([work[n][part, last] for n in range(len(SHARES))], 1)
+            for part in range(parts)
+        ],
+        0,
+    )
+    sums, total = unpacked(whole)
+    linear = [sums[back] / total for back in range(2)]
+    weighted = [
+        linear[back]
+        * (sums[2 + back] * sums[2 + back] + sums[4 + back] * sums[4 + back])
+        / (total * total)
+        for back in range(2)
+    ]
+    ordered = in_order(
+        *(jnp.concatenate([linear[back], weighted[back]], 0) for back in range(2)), turn[...]
+    )
+    lin_out[...] = ordered[: own * parts]
+    wgt_out[...] = ordered[own * parts :]
     mask_copy.wait_send()
     for day in range(days):
         direct(day).wait_send()
@@ -316,7 +376,6 @@
     own = rows // chips // parts
     steps = chips.bit_length() - 1
     streams = len(streams_of(steps, parts))
-    half = PACKED // 2
     stations = local * halves
     operands = (spectra, pair_list.T, mask, jnp.asarray(lag_table()))
     hbm = pl.BlockSpec(memory_space=pltpu.HBM)
@@ -328,16 +387,20 @@
         out_specs=[vmem, vmem],
         scratch_shapes=[
             pltpu.VMEM((2, days, stations, width), jnp.bfloat16),
-            pltpu.VMEM((2 * F, 2 * LANES), jnp.bfloat16),
+            pltpu.VMEM((F, 2 * WIDE), jnp.bfloat16),
             pltpu.VMEM((2, 2 * rows), jnp.int32),
             pltpu.VMEM((2, *mask.shape), jnp.int32),
             pltpu.VMEM((2 * rows, stations), jnp.float32),
             pltpu.VMEM((2, rows, stations), jnp.float32),
             pltpu.VMEM((rows, PACKED), jnp.float32),
-            pltpu.VMEM((3, rows, 128), jnp.float32),
-            pltpu.VMEM((streams, chips, own, half), jnp.float32),
-            pltpu.VMEM((streams, chips, own, half), jnp.bfloat16),
-            pltpu.VMEM((streams, chips, own, half), jnp.bfloat16),
+            pltpu.VMEM((6, rows, 128), jnp.float32),
+            pltpu.VMEM((rows, 128), jnp.float32),
+            pltpu.VMEM((WIDE, WIDE), jnp.bfloat16),
+            *(
+                pltpu.VMEM((parts, chips, own, share), dtype)
+                for dtype in (jnp.float32, jnp.bfloat16, jnp.bfloat16)
+                for share in SHARES
+            ),
             pltpu.SemaphoreType.DMA((4,)),
             pltpu.SemaphoreType.DMA((days, halves - 1)),
             pltpu.SemaphoreType.DMA((days, halves - 1)),

time: 35.4 us -> 36.1 us (1.020)
  Pallas kernels: 33.9 us -> 34.6 us
    pallas_call x1, Pallas kernels: 33.9 us -> 34.6 us  [per_device(): pl.pallas_call(functools.partial(kernel, chips, halves), out_shape=[jax.S...]
where the time goes in v4:
time: 36.1 us; the launch traced here: 35.9 us
  Pallas kernels  34.6 us (96%)
  local copies, waits for them, and re-layouts  0.66 us (2%)
  between operations  0.64 us (2%)
    pallas_call x1, Pallas kernels, per_device(): pl.pallas_call(functools.partial(kernel, chips, halves), out_shape=[jax.S...  34.6 us

profile of v4, /device:TPU:0, one launch (start us, length us, event | category | flops | bytes accessed | tf_op | source)
XLA Modules:
  0.0 35.9 jit_solution(7731369464062723045)
XLA Ops:
  0.6 34.6 %shard_map.59 = (f32[32,512]{1,0:T(8,128)S(1)}, f32[32,512]{1,0:T(8,128)S(1)}) custom-call(bf16[4,64,1024]{2,1,0:T(8,128)(2,1)} %spectra.1, s32[2,512]{1,0:T(2,128)} %bitcast.5, s32[4,128]{1,0:T(4,128)} %mask_hbm.1, bf16[512,512]{1,0:T(8,128)(2,1)} %constant.2.clone.table), custom_call_target="tpu_custom_call" | custom-call | tf_op jit(solution)/shard_map/pallas_call | solution.py:383
  35.2 0.7 %slice_bitcast_fusion = (f32[401,32]{0,1:T(8,128)}, f32[401,32]{0,1:T(8,128)}) fusion(f32[32,512]{1,0:T(8,128)S(1)} %get-tuple-element.5, f32[32,512]{1,0:T(8,128)S(1)} %get-tuple-element.4), kind=kLoop, calls=%fused_computation | loop fusion | bytes 205312 | tf_op jit(solution)/shard_map/transpose | solution.py:418

commit v5 on v4

--- a/solution.py
+++ b/solution.py
@@ -16,7 +16,8 @@
 LANES = 512
 WIDE = 256
 PACKED = 1280
-SHARES = (896, 384)
+SHARES = (384, 256, 384, 256)
+AHEAD = 2
 MESH = pl.DeviceIdType.MESH
 VMEM_LIMIT = 40 * 1024 * 1024
 
@@ -89,9 +90,9 @@
     straight = list(range(steps))
     swapped = straight[1::-1] + straight[2:]
     return [
-        (p, n, n * SHARES[0], SHARES[n], order)
+        (p, n, sum(SHARES[:n]), SHARES[n], swapped if n % 2 else straight)
         for p in range(parts)
-        for n, order in enumerate((straight, swapped))
+        for n in range(len(SHARES))
     ]
 
 
@@ -99,8 +100,9 @@
     chips, halves, spectra, pairs_hbm, mask_hbm, table, lin_out, wgt_out,
     spec_all, table_v, pairs, mask, hot, pick, acc, tail, count, turn, *boxes_and_semaphores,
 ):
-    work, outbox, inbox = (boxes_and_semaphores[2 * n : 2 * n + 2] for n in range(3))
-    load_sem, gsend, grecv, fsend, frecv, dsend, drecv, rsend, rrecv = boxes_and_semaphores[6:]
+    kinds = len(SHARES)
+    work, outbox, inbox = (boxes_and_semaphores[kinds * n : kinds * (n + 1)] for n in range(3))
+    load_sem, gsend, grecv, fsend, frecv, dsend, drecv, rsend, rrecv = boxes_and_semaphores[3 * kinds :]
     days, local, _ = spectra.shape
     rows = acc.shape[0]
     steps = chips.bit_length() - 1
@@ -182,8 +184,9 @@
     )
 
     for day in range(days):
-        for off in range(1, halves):
-            gather(day, off).start()
+        if day < AHEAD:
+            for off in range(1, halves):
+                gather(day, off).start()
         if day == 0:
             mask_copy.start()
         direct(day).start()
@@ -311,6 +314,12 @@
         for off in range(1, halves):
             gather(day, off).wait_recv()
             forward(day, off).start()
+
+        @pl.when(day + AHEAD < days)
+        def _():
+            for off in range(1, halves):
+                gather(day + AHEAD, off).start()
+
         correlate(core, day, 0, rows)
         direct(day).wait_recv()
         for off in range(1, halves):

time: 36.1 us -> 35 us (0.970)
  Pallas kernels: 34.6 us -> 33.5 us
    pallas_call x1, Pallas kernels: 34.6 us -> 33.5 us  [per_device(): pl.pallas_call(functools.partial(kernel, chips, halves), out_shape=[jax.S...]
where the time goes in v5:
time: 35 us; the launch traced here: 34.8 us
  Pallas kernels  33.5 us (96%)
  local copies, waits for them, and re-layouts  0.66 us (2%)
  between operations  0.64 us (2%)
    pallas_call x1, Pallas kernels, per_device(): pl.pallas_call(functools.partial(kernel, chips, halves), out_shape=[jax.S...  33.5 us

profile of v5, /device:TPU:0, one launch (start us, length us, event | category | flops | bytes accessed | tf_op | source)
XLA Modules:
  0.0 34.8 jit_solution(3327819500948800441)
XLA Ops:
  0.6 33.5 %shard_map.59 = (f32[32,512]{1,0:T(8,128)S(1)}, f32[32,512]{1,0:T(8,128)S(1)}) custom-call(bf16[4,64,1024]{2,1,0:T(8,128)(2,1)} %spectra.1, s32[2,512]{1,0:T(2,128)} %bitcast.5, s32[4,128]{1,0:T(4,128)} %mask_hbm.1, bf16[512,512]{1,0:T(8,128)(2,1)} %constant.2.clone.table), custom_call_target="tpu_custom_call" | custom-call | tf_op jit(solution)/shard_map/pallas_call | solution.py:392
  34.2 0.7 %slice_bitcast_fusion = (f32[401,32]{0,1:T(8,128)}, f32[401,32]{0,1:T(8,128)}) fusion(f32[32,512]{1,0:T(8,128)S(1)} %get-tuple-element.5, f32[32,512]{1,0:T(8,128)S(1)} %get-tuple-element.4), kind=kLoop, calls=%fused_computation | loop fusion | bytes 205312 | tf_op jit(solution)/shard_map/transpose | solution.py:427

commit v6 on v5

--- a/solution.py
+++ b/solution.py
@@ -16,7 +16,7 @@
 LANES = 512
 WIDE = 256
 PACKED = 1280
-SHARES = (384, 256, 384, 256)
+SHARES = (384, 128, 512, 256)
 AHEAD = 2
 MESH = pl.DeviceIdType.MESH
 VMEM_LIMIT = 40 * 1024 * 1024
@@ -335,37 +335,39 @@
     for part in range(parts):
         here = pl.ds(part * per_part, per_part)
         correlate(1 - core, days - 1, part * per_part, per_part)
-        acc[here, 6 * 128 :] = packed_rest([tail[j, here] for j in range(6)], count[here])
+        packed = False
         for s in range(len(streams)):
             if streams[s][0] == part:
+                if not packed and streams[s][2] + streams[s][3] > 6 * 128:
+                    acc[here, 6 * 128 :] = packed_rest([tail[j, here] for j in range(6)], count[here])
+                    packed = True
                 send(s, 0)
+
+    def finish(part):
+        whole = jnp.concatenate([work[n][part, chips - 2] for n in range(len(SHARES))], 1)
+        sums, total = unpacked(whole)
+        linear = [sums[back] / total for back in range(2)]
+        weighted = [
+            linear[back]
+            * (sums[2 + back] * sums[2 + back] + sums[4 + back] * sums[4 + back])
+            / (total * total)
+            for back in range(2)
+        ]
+        ordered = in_order(
+            *(jnp.concatenate([linear[back], weighted[back]], 0) for back in range(2)), turn[...]
+        )
+        here = pl.ds(part * own, own)
+        lin_out[here] = ordered[:own]
+        wgt_out[here] = ordered[own:]
+
     for k in range(steps):
         for s in range(len(streams)):
             receive(s, k)
             if k + 1 < steps:
                 send(s, k + 1)
-
-    last = chips - 2
-    whole = jnp.concatenate(
-        [
-            jnp.concatenate([work[n][part, last] for n in range(len(SHARES))], 1)
-            for part in range(parts)
-        ],
-        0,
-    )
-    sums, total = unpacked(whole)
-    linear = [sums[back] / total for back in range(2)]
-    weighted = [
-        linear[back]
-        * (sums[2 + back] * sums[2 + back] + sums[4 + back] * sums[4 + back])
-        / (total * total)
-        for back in range(2)
-    ]
-    ordered = in_order(
-        *(jnp.concatenate([linear[back], weighted[back]], 0) for back in range(2)), turn[...]
-    )
-    lin_out[...] = ordered[: own * parts]
-    wgt_out[...] = ordered[own * parts :]
+            elif s + 1 == len(streams) or streams[s + 1][0] != streams[s][0]:
+                finish(streams[s][0])
+
     mask_copy.wait_send()
     for day in range(days):
         direct(day).wait_send()

time: 35 us -> 35.7 us (1.020)
  Pallas kernels: 33.5 us -> 34.3 us
    pallas_call x1, Pallas kernels: 33.5 us -> 34.3 us  [per_device(): pl.pallas_call(functools.partial(kernel, chips, halves), out_shape=[jax.S...]
where the time goes in v6:
time: 35.7 us; the launch traced here: 35.5 us
  Pallas kernels  34.3 us (96%)
  local copies, waits for them, and re-layouts  0.66 us (2%)
  between operations  0.64 us (2%)
    pallas_call x1, Pallas kernels, per_device(): pl.pallas_call(functools.partial(kernel, chips, halves), out_shape=[jax.S...  34.3 us

profile of v6, /device:TPU:0, one launch (start us, length us, event | category | flops | bytes accessed | tf_op | source)
XLA Modules:
  0.0 35.5 jit_solution(5687427590529957059)
XLA Ops:
  0.6 34.3 %shard_map.59 = (f32[32,512]{1,0:T(8,128)S(1)}, f32[32,512]{1,0:T(8,128)S(1)}) custom-call(bf16[4,64,1024]{2,1,0:T(8,128)(2,1)} %spectra.1, s32[2,512]{1,0:T(2,128)} %bitcast.5, s32[4,128]{1,0:T(4,128)} %mask_hbm.1, bf16[512,512]{1,0:T(8,128)(2,1)} %constant.2.clone.table), custom_call_target="tpu_custom_call" | custom-call | tf_op jit(solution)/shard_map/pallas_call | solution.py:394
  34.9 0.7 %slice_bitcast_fusion = (f32[401,32]{0,1:T(8,128)}, f32[401,32]{0,1:T(8,128)}) fusion(f32[32,512]{1,0:T(8,128)S(1)} %get-tuple-element.5, f32[32,512]{1,0:T(8,128)S(1)} %get-tuple-element.4), kind=kLoop, calls=%fused_computation | loop fusion | bytes 205312 | tf_op jit(solution)/shard_map/transpose | solution.py:429

commit v7 on v6

--- a/solution.py
+++ b/solution.py
@@ -16,7 +16,7 @@
 LANES = 512
 WIDE = 256
 PACKED = 1280
-SHARES = (384, 128, 512, 256)
+SHARES = (256, 384, 256, 384)
 AHEAD = 2
 MESH = pl.DeviceIdType.MESH
 VMEM_LIMIT = 40 * 1024 * 1024

time: 35.7 us -> 34.7 us (0.972)
  Pallas kernels: 34.3 us -> 33.3 us
    pallas_call x1, Pallas kernels: 34.3 us -> 33.3 us  [per_device(): pl.pallas_call(functools.partial(kernel, chips, halves), out_shape=[jax.S...]
where the time goes in v7:
time: 34.7 us; the launch traced here: 34.6 us
  Pallas kernels  33.3 us (96%)
  local copies, waits for them, and re-layouts  0.66 us (2%)
  between operations  0.64 us (2%)
    pallas_call x1, Pallas kernels, per_device(): pl.pallas_call(functools.partial(kernel, chips, halves), out_shape=[jax.S...  33.3 us

profile of v7, /device:TPU:0, one launch (start us, length us, event | category | flops | bytes accessed | tf_op | source)
XLA Modules:
  0.0 34.6 jit_solution(4583815407675676379)
XLA Ops:
  0.6 33.3 %shard_map.59 = (f32[32,512]{1,0:T(8,128)S(1)}, f32[32,512]{1,0:T(8,128)S(1)}) custom-call(bf16[4,64,1024]{2,1,0:T(8,128)(2,1)} %spectra.1, s32[2,512]{1,0:T(2,128)} %bitcast.5, s32[4,128]{1,0:T(4,128)} %mask_hbm.1, bf16[512,512]{1,0:T(8,128)(2,1)} %constant.2.clone.table), custom_call_target="tpu_custom_call" | custom-call | tf_op jit(solution)/shard_map/pallas_call | solution.py:394
  33.9 0.7 %slice_bitcast_fusion = (f32[401,32]{0,1:T(8,128)}, f32[401,32]{0,1:T(8,128)}) fusion(f32[32,512]{1,0:T(8,128)S(1)} %get-tuple-element.5, f32[32,512]{1,0:T(8,128)S(1)} %get-tuple-element.4), kind=kLoop, calls=%fused_computation | loop fusion | bytes 205312 | tf_op jit(solution)/shard_map/transpose | solution.py:429

commit v8 on v7

--- a/solution.py
+++ b/solution.py
@@ -16,8 +16,8 @@
 LANES = 512
 WIDE = 256
 PACKED = 1280
-SHARES = (256, 384, 256, 384)
-AHEAD = 2
+SHARES = (384, 384, 256, 256)
+AHEAD = 3
 MESH = pl.DeviceIdType.MESH
 VMEM_LIMIT = 40 * 1024 * 1024
 

time: 34.7 us -> 34 us (0.980)
  Pallas kernels: 33.3 us -> 32.5 us
    pallas_call x1, Pallas kernels: 33.3 us -> 32.5 us  [per_device(): pl.pallas_call(functools.partial(kernel, chips, halves), out_shape=[jax.S...]
where the time goes in v8:
time: 34 us; the launch traced here: 33.8 us
  Pallas kernels  32.5 us (96%)
  local copies, waits for them, and re-layouts  0.66 us (2%)
  between operations  0.64 us (2%)
    pallas_call x1, Pallas kernels, per_device(): pl.pallas_call(functools.partial(kernel, chips, halves), out_shape=[jax.S...  32.5 us

profile of v8, /device:TPU:0, one launch (start us, length us, event | category | flops | bytes accessed | tf_op | source)
XLA Modules:
  0.0 33.8 jit_solution(14193468840566458127)
XLA Ops:
  0.6 32.5 %shard_map.59 = (f32[32,512]{1,0:T(8,128)S(1)}, f32[32,512]{1,0:T(8,128)S(1)}) custom-call(bf16[4,64,1024]{2,1,0:T(8,128)(2,1)} %spectra.1, s32[2,512]{1,0:T(2,128)} %bitcast.5, s32[4,128]{1,0:T(4,128)} %mask_hbm.1, bf16[512,512]{1,0:T(8,128)(2,1)} %constant.2.clone.table), custom_call_target="tpu_custom_call" | custom-call | tf_op jit(solution)/shard_map/pallas_call | solution.py:394
  33.2 0.7 %slice_bitcast_fusion = (f32[401,32]{0,1:T(8,128)}, f32[401,32]{0,1:T(8,128)}) fusion(f32[32,512]{1,0:T(8,128)S(1)} %get-tuple-element.5, f32[32,512]{1,0:T(8,128)S(1)} %get-tuple-element.4), kind=kLoop, calls=%fused_computation | loop fusion | bytes 205312 | tf_op jit(solution)/shard_map/transpose | solution.py:429

commit v9 on v8

--- a/solution.py
+++ b/solution.py
@@ -17,7 +17,7 @@
 WIDE = 256
 PACKED = 1280
 SHARES = (384, 384, 256, 256)
-AHEAD = 3
+AHEAD = 4
 MESH = pl.DeviceIdType.MESH
 VMEM_LIMIT = 40 * 1024 * 1024
 

time: 34 us -> 34 us (level)
  no operation moved by 1% of the time
where the time goes in v9:
time: 34 us; the launch traced here: 33.8 us
  Pallas kernels  32.5 us (96%)
  local copies, waits for them, and re-layouts  0.66 us (2%)
  between operations  0.64 us (2%)
    pallas_call x1, Pallas kernels, per_device(): pl.pallas_call(functools.partial(kernel, chips, halves), out_shape=[jax.S...  32.5 us

profile of v9, /device:TPU:0, one launch (start us, length us, event | category | flops | bytes accessed | tf_op | source)
XLA Modules:
  0.0 33.8 jit_solution(3360517603001549263)
XLA Ops:
  0.6 32.5 %shard_map.59 = (f32[32,512]{1,0:T(8,128)S(1)}, f32[32,512]{1,0:T(8,128)S(1)}) custom-call(bf16[4,64,1024]{2,1,0:T(8,128)(2,1)} %spectra.1, s32[2,512]{1,0:T(2,128)} %bitcast.5, s32[4,128]{1,0:T(4,128)} %mask_hbm.1, bf16[512,512]{1,0:T(8,128)(2,1)} %constant.2.clone.table), custom_call_target="tpu_custom_call" | custom-call | tf_op jit(solution)/shard_map/pallas_call | solution.py:394
  33.2 0.7 %slice_bitcast_fusion = (f32[401,32]{0,1:T(8,128)}, f32[401,32]{0,1:T(8,128)}) fusion(f32[32,512]{1,0:T(8,128)S(1)} %get-tuple-element.5, f32[32,512]{1,0:T(8,128)S(1)} %get-tuple-element.4), kind=kLoop, calls=%fused_computation | loop fusion | bytes 205312 | tf_op jit(solution)/shard_map/transpose | solution.py:429
